TPU v7x, 32 devices: a whole 2x2x4 slice. The times are simulated.
32 devices in a mesh: row: 4 (over y, core), col: 8 (over z, x).
Axes of the slice: x: 2, y: 2, z: 4, core: 2. Of those that a mesh axis runs over, the one named last changes fastest.
Arguments:
- factors: float32 [2, 96, 49152], P(None, 'row', 'col'), may hold values from -0.3125 to 0.3125
- covariance: float32 [12288, 12288], P('row', 'col'), may hold values from -26 to 26, as said below
- noise: float32 [12288, 12288], P('row', 'col'), may hold values from -2.4 to 2.4
- positions: float32 [12288], replicated, may hold values from 0 to 1
Outputs:
- forecast: float32 [12288, 12288], P('row', 'col')
Inputs may be any that keep to these rules, and one draw needn't show every extreme that they name: covariance is symmetric, with 2 added on its diagonal.
All inputs are finite; a program needn't handle non-finite values.
Results may differ from a plain program's by a relative error of at most 0.00014.
Values sent between devices are 32-bit elements; how exact they have to be, the bound alone decides.
A program may use at most 256 MiB of HBM per device.

v0:
```python
import jax
import jax.numpy as jnp
from jax import lax
from jax.sharding import PartitionSpec as P

B = 128


def padded_2(cells, sides, width):
    for axis, dim in sides:
        count = lax.axis_size(axis)
        ends = count - 1
        head = lax.slice_in_dim(cells, 0, width, axis=dim)
        tail = lax.slice_in_dim(cells, cells.shape[dim] - width, cells.shape[dim], axis=dim)
        cells = jnp.concatenate(
            [
                lax.ppermute(tail, axis, [(i, (i + 1) % count) for i in range(ends)]),
                cells,
                lax.ppermute(head, axis, [((i + 1) % count, i) for i in range(ends)]),
            ],
            axis=dim,
        )
    return cells


def spread(block, axis, owner):
    block = jnp.where(lax.axis_index(axis) == owner, block, jnp.zeros_like(block))
    return lax.psum(block, axis)


def left_local(blocks, padded, reach):
    count = blocks.shape[0]
    size = blocks.shape[2]
    width = padded.shape[1]
    split = padded.reshape(count + 2 * reach, size, width)
    total = jnp.zeros((count, size, width), jnp.float32)
    for offset in range(2 * reach + 1):
        total = total + jnp.einsum(
            "iab,ibk->iak",
            blocks[:, offset],
            split[offset : offset + count],
            precision=lax.Precision.HIGHEST,
        )
    return total.reshape(count * size, width)


def right_local(blocks, padded, reach):
    count = blocks.shape[0]
    size = blocks.shape[2]
    height = padded.shape[0]
    split = padded.reshape(height, count + 2 * reach, size)
    total = jnp.zeros((height, count, size), jnp.float32)
    for offset in range(2 * reach + 1):
        total = total + jnp.einsum(
            "kib,iab->kia",
            split[:, offset : offset + count],
            blocks[:, offset],
            precision=lax.Precision.HIGHEST,
        )
    return total.reshape(height, count * size)


def block_product(first, second):
    return jnp.einsum("iab,ibc->iac", first, second, precision=lax.Precision.HIGHEST)


def compose(second, rimmed):
    lower = rimmed[:-2]
    middle = rimmed[1:-1]
    upper = rimmed[2:]
    far_low = block_product(second[:, 0], lower[:, 0])
    near_low = block_product(second[:, 0], lower[:, 1]) + block_product(second[:, 1], middle[:, 0])
    centre = (
        block_product(second[:, 0], lower[:, 2])
        + block_product(second[:, 1], middle[:, 1])
        + block_product(second[:, 2], upper[:, 0])
    )
    near_high = block_product(second[:, 1], middle[:, 2]) + block_product(second[:, 2], upper[:, 1])
    far_high = block_product(second[:, 2], upper[:, 2])
    return jnp.stack([far_low, near_low, centre, near_high, far_high], axis=1)


def body(factors, covariance, noise, positions):
    gathered = lax.all_gather(factors, "col", axis=2, tiled=True)
    block_rows = gathered.shape[1]
    bsize = B
    whole = gathered.reshape(2, block_rows, 3, bsize, bsize)
    rows_here = covariance.shape[0]
    cols_here = covariance.shape[1]
    block_cols = cols_here // bsize
    col_at = lax.axis_index("col")
    row_at = lax.axis_index("row")
    source = col_at * block_cols // block_rows
    start = col_at * block_cols % block_rows
    rimmed = padded_2(whole[0], (("row", 0),), 1)
    composed = compose(whole[1], rimmed)
    padded = padded_2(covariance, (("row", 0),), 2 * bsize)
    tile = left_local(composed, padded, 2)
    selected = lax.dynamic_slice_in_dim(composed, start, block_cols, 0)
    matching = spread(selected, "row", source)
    padded = padded_2(tile, (("col", 1),), 2 * bsize)
    tile = right_local(matching, padded, 2)
    row_places = lax.dynamic_slice_in_dim(positions, row_at * rows_here, rows_here, 0)
    col_places = lax.dynamic_slice_in_dim(positions, col_at * cols_here, cols_here, 0)
    distance = (row_places[:, None] - col_places[None, :]) / 0.5
    taper = jnp.exp(-distance * distance)
    return tile * taper + noise


def solution(mesh):
    placed = (P(None, "row", "col"), P("row", "col"), P("row", "col"), P())
    return jax.shard_map(
        body, mesh=mesh, in_specs=placed, out_specs=P("row", "col"), check_vma=False
    )
```

profile of v0, /device:TPU:17, one launch (start us, length us, event | category | flops | bytes accessed | tf_op | source)
XLA Modules:
  0.0 694.8 jit_solution(4363868356630533710)
XLA Ops:
  15.0 15.4 %collective-permute-done.2 = f32[256,1536]{1,0:T(8,128)S(1)} collective-permute-done((f32[256,1536]{1,0:T(8,128)S(1)}, f32[256,1536]{1,0:T(8,128)S(1)}, u32[]{:S(2)}, u32[]{:S(2)}) %collective-permute-start.2) | collective-permute-done | bytes 1572896 | tf_op jit(solution)/shard_map/ppermute | solution.py:17
  31.7 14.2 %constant_dynamic-update-slice_fusion = (f32[3328,1536]{1,0:T(8,128)}, f32[3328,1536]{1,0:T(8,128)S(1)}) fusion(f32[3328,1536]{1,0:T(8,128)} %constant_dynamic-update-slice_fusion.1, f32[3072,1536]{1,0:T(8,128)} %param.5), kind=kLoop, calls=%fused_computation.67 | loop fusion | bytes 56623104 | tf_op jit(solution)/shard_map/concatenate | solution.py:15
  46.1 26.8 %fusion.44 = (f32[3072,1536]{1,0:T(8,128)}, f32[3072,1536]{1,0:T(8,128)}) fusion(f32[3328,1536]{1,0:T(8,128)} %get-tuple-element.11), kind=kLoop, calls=%fused_computation.77 | loop fusion | bytes 75497472 | tf_op jit(solution)/shard_map/slice | solution.py:41
  72.9 12.9 %fusion.45 = (f32[3072,1536]{1,0:T(8,128)}, f32[3072,1536]{1,0:T(8,128)}) fusion(f32[3328,1536]{1,0:T(8,128)S(1)} %constant_dynamic-update-slice_fusion.2), kind=kLoop, calls=%fused_computation.78 | loop fusion | bytes 75497472 | tf_op jit(solution)/shard_map/slice | solution.py:41
  85.8 61.6 %all-gather.2.cloned.1.call-done = f32[2,24,49152]{2,1,0:T(8,128)} async-done(((f32[2,24,6144]{2,1,0:T(8,128)}), f32[2,24,49152]{2,1,0:T(8,128)}) %all-gather.2.cloned.1.call-update) | async-done | bytes 9437200 | tf_op jit(solution)/shard_map/all_gather | solution.py:84
  159.0 6.1 copy.23
  174.9 4.7 fusion.20
  179.7 4.9 bitcast_dynamic-update-slice_fusion.1
  198.0 22.8 %fusion.51 = f32[24,128,1536]{2,1,0:T(8,128)} fusion(f32[24,128,128]{1,2,0:T(8,128)S(1)} %get-tuple-element.24, f32[24,128,1536]{2,1,0:T(8,128)} %bitcast.158), kind=kOutput, calls=%fused_computation.84 | convolution fusion | flops 7247757312 | bytes 39321600 | tf_op jit(solution)/shard_map/iab,ibk->iak/dot_general | solution.py:38
  220.8 22.6 %fusion.50 = f32[24,128,1536]{2,1,0:T(8,128)} fusion(f32[24,128,128]{1,2,0:T(8,128)S(1)} %get-tuple-element.22, f32[24,128,1536]{2,1,0:T(8,128)} %bitcast.163), kind=kOutput, calls=%fused_computation.83 | convolution fusion | flops 7247757312 | bytes 39321600 | tf_op jit(solution)/shard_map/iab,ibk->iak/dot_general | solution.py:38
  243.4 22.9 %fusion.49 = f32[24,128,1536]{2,1,0:T(8,128)} fusion(f32[24,128,128]{2,1,0:T(8,128)S(1)} %get-tuple-element.20, f32[24,128,1536]{2,1,0:T(8,128)} %bitcast.162), kind=kOutput, calls=%fused_computation.82 | convolution fusion | flops 7247757312 | bytes 39321600 | tf_op jit(solution)/shard_map/iab,ibk->iak/dot_general | solution.py:38
  271.0 23.0 %fusion.52 = f32[24,128,1536]{2,1,0:T(8,128)} fusion(f32[24,128,128]{1,2,0:T(8,128)S(1)} %get-tuple-element.26, f32[24,128,1536]{2,1,0:T(8,128)} %bitcast.161), kind=kOutput, calls=%fused_computation.85 | convolution fusion | flops 7247757312 | bytes 39321600 | tf_op jit(solution)/shard_map/iab,ibk->iak/dot_general | solution.py:38
  298.5 38.2 %add_add_fusion.1 = f32[24,128,1536]{2,1,0:T(8,128)} fusion(f32[24,128,1536]{2,1,0:T(8,128)} %fusion.52, f32[24,128,1536]{2,1,0:T(8,128)} %fusion.51, f32[24,128,1536]{2,1,0:T(8,128)} %fusion.49, f32[24,128,1536]{2,1,0:T(8,128)} %fusion.50, f32[24,128,128]{2,1,0:T(8,128)S(1)} %get-tuple-element.28, f32[24,128,1536]{2,1,0:T(8,128)} %bitcast.160), kind=kOutput, calls=%fused_computation.16 | convolution fusion | flops 7266631680 | bytes 114819072 | tf_op jit(solution)/shard_map/iab,ibk->iak/dot_general | solution.py:38
  336.8 18.6 %copy.40 = f32[3072,1536]{0,1:T(8,128)} copy(f32[3072,1536]{1,0:T(8,128)} %bitcast.159) | data formatting | bytes 37748736 | tf_op jit(solution)/shard_map/reshape | solution.py:44
  355.3 6.3 fusion.46
  372.6 126.8 %collective-permute-done.4 = f32[3072,256]{0,1:T(8,128)S(1)} collective-permute-done((f32[3072,256]{0,1:T(8,128)}, f32[3072,256]{0,1:T(8,128)S(1)}, u32[]{:S(2)}, u32[]{:S(2)}) %collective-permute-start.4) | collective-permute-done | bytes 3145760 | tf_op jit(solution)/shard_map/ppermute | solution.py:17
  502.2 16.5 %pad_maximum_fusion = f32[3072,2048]{0,1:T(8,128)} fusion(f32[3072,256]{0,1:T(8,128)} %collective-permute-done.5, f32[3072,1536]{0,1:T(8,128)} %copy.40, f32[3072,256]{0,1:T(8,128)S(1)} %collective-permute-done.4), kind=kLoop, calls=%fused_computation.1 | loop fusion | flops 12582912 | bytes 50331648 | tf_op jit(solution)/shard_map/concatenate | solution.py:15
  518.6 23.0 %fusion.5 = f32[12,128,3072]{2,1,0:T(8,128)} fusion(f32[3072,16,128]{0,2,1:T(8,128)} %bitcast.153, f32[12,5,128,128]{2,3,0,1:T(8,128)} %all-reduce.2.cloned.1.call-done), kind=kOutput, calls=%fused_computation.7 | convolution fusion | flops 7247757312 | bytes 38535168 | tf_op jit(solution)/shard_map/kib,iab->kia/dot_general | solution.py:54
  541.6 22.7 %fusion.7 = f32[12,128,3072]{2,1,0:T(8,128)} fusion(f32[3072,16,128]{0,2,1:T(8,128)} %bitcast.154, f32[12,5,128,128]{2,3,0,1:T(8,128)S(1)} %copy-done.3), kind=kOutput, calls=%fused_computation.9 | convolution fusion | flops 7247757312 | bytes 38535168 | tf_op jit(solution)/shard_map/kib,iab->kia/dot_general | solution.py:54
  564.3 22.5 %fusion.9 = f32[12,128,3072]{2,1,0:T(8,128)} fusion(f32[3072,16,128]{0,2,1:T(8,128)} %bitcast.155, f32[12,5,128,128]{2,3,0,1:T(8,128)S(1)} %copy-done.3), kind=kOutput, calls=%fused_computation.11 | convolution fusion | flops 7247757312 | bytes 38535168 | tf_op jit(solution)/shard_map/kib,iab->kia/dot_general | solution.py:54
  586.8 22.7 %fusion.11 = f32[12,128,3072]{2,1,0:T(8,128)} fusion(f32[3072,16,128]{0,2,1:T(8,128)} %bitcast.156, f32[12,5,128,128]{2,3,0,1:T(8,128)S(1)} %copy-done.3), kind=kOutput, calls=%fused_computation.13 | convolution fusion | flops 7247757312 | bytes 38535168 | tf_op jit(solution)/shard_map/kib,iab->kia/dot_general | solution.py:54
  609.5 38.5 %add_add_fusion = f32[12,128,3072]{2,1,0:T(8,128)} fusion(f32[12,128,3072]{2,1,0:T(8,128)} %fusion.5, f32[12,128,3072]{2,1,0:T(8,128)} %fusion.7, f32[12,128,3072]{2,1,0:T(8,128)} %fusion.11, f32[12,128,3072]{2,1,0:T(8,128)} %fusion.9, f32[3072,16,128]{0,2,1:T(8,128)} %bitcast.157, f32[12,5,128,128]{2,3,0,1:T(8,128)} %all-reduce.2.cloned.1.call-done), kind=kOutput, calls=%fused_computation.15 | convolution fusion | flops 7266631680 | bytes 114032640 | tf_op jit(solution)/shard_map/kib,iab->kia/dot_general | solution.py:54
  648.0 18.7 %copy.53 = f32[3072,1536]{1,0:T(8,128)} copy(f32[3072,1536]{0,1:T(8,128)} %bitcast.164) | data formatting | bytes 37748736 | tf_op jit(solution)/shard_map/reshape | solution.py:60
  666.6 20.9 %fusion.2 = f32[3072,1536]{1,0:T(8,128)} fusion(f32[3072,1536]{1,0:T(8,128)} %param.6, f32[3072,1536]{1,0:T(8,128)} %copy.53, f32[1536]{0:T(1024)S(1)} %dynamic_slice.11, f32[3072]{0:T(1024)S(1)} %dynamic-slice-done), kind=kLoop, calls=%fused_computation.4 | loop fusion | flops 28311552 | bytes 56641536 | tf_op jit(solution)/shard_map/add | solution.py:107
  (52 shorter events, 67.5 us)
Async XLA Ops:
  6.5 140.9 %all-gather.2.cloned.1.call-start = ((), (), s32[]{:S(2)}) async-start(), calls=%async_computation | async-start | bytes 10616832 | tf_op jit(solution)/shard_map/all_gather | solution.py:84
  7.3 511.4 %all-reduce.2.cloned.1.call-start = ((), (), s32[]{:S(2)}) async-start(), calls=%async_computation.1 | async-start | bytes 7864320 | tf_op jit(solution)/shard_map/psum | solution.py:28
  9.4 21.1 %collective-permute-start.2 = (f32[256,1536]{1,0:T(8,128)S(1)}, f32[256,1536]{1,0:T(8,128)S(1)}, u32[]{:S(2)}, u32[]{:S(2)}) collective-permute-start(f32[256,1536]{1,0:T(8,128)S(1)} %get-tuple-element.13), channel_id=1, source_target_pairs={{0,8},{8,16},{16,24},{1,9},{9,17},{17,25},{2,10},{10,18},{18,26},{... | collective-permute-start | bytes 4718600 | tf_op jit(solution)/shard_map/ppermute | solution.py:17
  13.1 32.8 %collective-permute-start.3 = (f32[256,1536]{1,0:T(8,128)S(1)}, f32[256,1536]{1,0:T(8,128)S(1)}, u32[]{:S(2)}, u32[]{:S(2)}) collective-permute-start(f32[256,1536]{1,0:T(8,128)S(1)} %get-tuple-element.14), channel_id=1, source_target_pairs={{8,0},{16,8},{24,16},{9,1},{17,9},{25,17},{10,2},{18,10},{26,18},{... | collective-permute-start | bytes 4718600 | tf_op jit(solution)/shard_map/ppermute | solution.py:19
  152.6 3.5 copy-start.1
  153.4 2.9 copy-start.2
  168.2 11.5 %copy-start = (f32[24,3,128,128]{2,3,0,1:T(8,128)S(1)}, f32[24,3,128,128]{2,3,0,1:T(8,128)}, u32[]{:S(2)}) copy-start(f32[24,3,128,128]{2,3,0,1:T(8,128)} %copy.23) | copy-start | bytes 14155780
  168.2 23.2 %collective-permute-start.1 = (f32[1,3,128,128]{2,3,0,1:T(8,128)S(1)}, f32[1,3,128,128]{2,3,0,1:T(8,128)S(1)}, u32[]{:S(2)}, u32[]{:S(2)}) collective-permute-start(f32[1,3,128,128]{2,3,0,1:T(8,128)S(1)} %copy.30), channel_id=1, source_target_pairs={{8,0},{16,8},{24,16},{9,1},{17,9},{25,17},{10,2},{18,10},{26,18},{... | collective-permute-start | bytes 589832 | tf_op jit(solution)/shard_map/ppermute | solution.py:19
  171.5 8.2 %collective-permute-start = (f32[1,3,128,128]{2,3,0,1:T(8,128)}, f32[1,3,128,128]{2,3,0,1:T(8,128)S(1)}, u32[]{:S(2)}, u32[]{:S(2)}) collective-permute-start(f32[1,3,128,128]{2,3,0,1:T(8,128)} %copy.22), channel_id=1, source_target_pairs={{0,8},{8,16},{16,24},{1,9},{9,17},{17,25},{2,10},{10,18},{18,26},{... | collective-permute-start | bytes 589832 | tf_op jit(solution)/shard_map/ppermute | solution.py:17
  174.9 9.6 %slice-start = ((s8[4718592]{0:T(1024)(128)(4,1)}), s8[4194304]{0:T(1024)(128)(4,1)S(1)}, s32[]{:S(2)}) async-start(s8[4718592]{0:T(1024)(128)(4,1)} %bitcast.169), calls=%async_computation.2 | async-start | bytes 8388608
  179.6 4.9 slice-start.1
  194.8 3.2 copy-start.4
  361.7 137.7 %collective-permute-start.4 = (f32[3072,256]{0,1:T(8,128)}, f32[3072,256]{0,1:T(8,128)S(1)}, u32[]{:S(2)}, u32[]{:S(2)}) collective-permute-start(f32[3072,256]{0,1:T(8,128)} %get-tuple-element.9), channel_id=1, source_target_pairs={{0,1},{1,2},{2,3},{3,4},{4,5},{5,6},{6,7},{8,9},{9,10},{10,11},{11... | collective-permute-start | bytes 9437192 | tf_op jit(solution)/shard_map/ppermute | solution.py:17
  363.9 138.3 %collective-permute-start.5 = (f32[3072,256]{0,1:T(8,128)}, f32[3072,256]{0,1:T(8,128)}, u32[]{:S(2)}, u32[]{:S(2)}) collective-permute-start(f32[3072,256]{0,1:T(8,128)} %get-tuple-element.10), channel_id=1, source_target_pairs={{1,0},{2,1},{3,2},{4,3},{5,4},{6,5},{7,6},{9,8},{10,9},{11,10},{12... | collective-permute-start | bytes 9437192 | tf_op jit(solution)/shard_map/ppermute | solution.py:19
  367.9 4.6 copy-start.5
  518.6 23.0 %copy-start.3 = (f32[12,5,128,128]{2,3,0,1:T(8,128)S(1)}, f32[12,5,128,128]{2,3,0,1:T(8,128)}, u32[]{:S(2)}) copy-start(f32[12,5,128,128]{2,3,0,1:T(8,128)} %all-reduce.2.cloned.1.call-done) | copy-start | bytes 11796484
  648.0 18.7 %dynamic-slice-start = ((f32[12288]{0:T(1024)}, s32[]{:T(128)}), f32[3072]{0:T(1024)S(1)}, s32[]{:S(2)}) async-start(f32[12288]{0:T(1024)} %param.7, s32[]{:T(128)} %select_n.33), calls=%async_computation.4 | async-start | bytes 25088 | tf_op jit(solution)/shard_map/dynamic_slice | solution.py:103
Sparse Core Ops, SparseCore 0:
  9.5 137.8 all-gather.1
  372.6 80.0 all-reduce.1
where the time goes:
time: 704 us; the launch traced here: 695 us
  matrix products  293 us (42%)
  waiting for transfers between devices  207 us (29%)
  local copies, waits for them, and re-layouts  120 us (17%)
  other arithmetic  41.9 us (6%)
  starting transfers between devices  18.6 us (3%)
  between operations  14.1 us (2%)
    ppermute x3, waiting for transfers between devices, padded_2(): lax.ppermute(tail, axis, [(i, (i + 1) % count) for i in range(ends)])  142 us
    dot_general x5, matrix products, left_local(): jnp.einsum('iab,ibk->iak', blocks[:, offset], split[offset:offset + count...  130 us
    dot_general x5, matrix products, right_local(): jnp.einsum('kib,iab->kia', split[:, offset:offset + count], blocks[:, off...  129 us
    all_gather x1, waiting for transfers between devices, body(): gathered = lax.all_gather(factors, 'col', axis=2, tiled=True)  61.6 us
    slice x2, local copies, waits for them, and re-layouts, left_local(): split[offset:offset + count]  39.7 us
    dot_general x9, matrix products, block_product(): jnp.einsum('iab,ibc->iac', first, second, precision=lax.Precision.HIGHEST)  34.3 us
    add x1, other arithmetic, body(): return tile * taper + noise  20.9 us
    reshape x1, local copies, waits for them, and re-layouts, right_local(): return total.reshape(height, count * size)  18.7 us
  transfers between devices with their start and end apart: 8, of which 4 were waited for; matrix products, arithmetic and copies ran while one was open for 14% of the time, Pallas kernels for 0%

commit v1 on v0

v1 whole, which is shorter than its diff:
```python
import functools

import jax
import jax.numpy as jnp
from jax import lax
from jax.experimental import pallas as pl
from jax.experimental.pallas import tpu as pltpu
from jax.sharding import PartitionSpec as P

B = 128
VMEM = 56 * 1024 * 1024


def parts(x):
    high = x.astype(jnp.bfloat16)
    return high, (x - high.astype(jnp.float32)).astype(jnp.bfloat16)


def dot(a, b):
    return jnp.dot(a, b, preferred_element_type=jnp.float32)


def neighbours(first, last, axis):
    count = lax.axis_size(axis)
    before = lax.ppermute(last, axis, [(i, i + 1) for i in range(count - 1)])
    after = lax.ppermute(first, axis, [(i + 1, i) for i in range(count - 1)])
    return before, after


def compose_kernel(f1, f2, low, high, band, compact, b1h, b1l, b2h, b2l):
    g = pl.program_id(0)
    rows = f1.shape[0]

    @pl.when(g == 0)
    def _():
        for ref in (b1h, b1l, b2h, b2l):
            ref[...] = jnp.zeros_like(ref)

    for r in range(2):
        for k in range(3):
            h, l = parts(f2[2 * g + r, k * B : (k + 1) * B, :])
            at = (slice(r * B, (r + 1) * B), slice((r + k) * B, (r + k + 1) * B))
            b2h[at] = h
            b2l[at] = l
    for j in range(4):
        for k in range(3):
            cut = slice(k * B, (k + 1) * B)
            if j == 0:
                x = jnp.where(g == 0, low[0, cut, :], f1[jnp.maximum(2 * g - 1, 0), cut, :])
            elif j == 3:
                x = jnp.where(
                    g == rows // 2 - 1, high[0, cut, :], f1[jnp.minimum(2 * g + 2, rows - 1), cut, :]
                )
            else:
                x = f1[2 * g + j - 1, cut, :]
            h, l = parts(x)
            at = (slice(j * B, (j + 1) * B), slice((j + k) * B, (j + k + 1) * B))
            b1h[at] = h
            b1l[at] = l
    c = dot(b2h[...], b1h[...]) + dot(b2h[...], b1l[...]) + dot(b2l[...], b1h[...])
    h, l = parts(c)
    band[0, : 2 * B, :] = h
    band[0, 2 * B :, :] = l
    compact[0] = c[:B, : 5 * B]
    compact[1] = c[B:, B:]


def compose(f1, f2, low, high):
    rows = f1.shape[0]
    whole = pl.BlockSpec(f1.shape, lambda g: (0, 0, 0))
    rim = pl.BlockSpec(low.shape, lambda g: (0, 0, 0))
    return pl.pallas_call(
        compose_kernel,
        grid=(rows // 2,),
        in_specs=[whole, whole, rim, rim],
        out_specs=[
            pl.BlockSpec((1, 4 * B, 6 * B), lambda g: (g, 0, 0)),
            pl.BlockSpec((2, B, 5 * B), lambda g: (g, 0, 0)),
        ],
        out_shape=[
            jax.ShapeDtypeStruct((rows // 2, 4 * B, 6 * B), jnp.bfloat16),
            jax.ShapeDtypeStruct((rows, B, 5 * B), jnp.float32),
        ],
        scratch_shapes=[
            pltpu.VMEM((4 * B, 6 * B), jnp.bfloat16),
            pltpu.VMEM((4 * B, 6 * B), jnp.bfloat16),
            pltpu.VMEM((2 * B, 4 * B), jnp.bfloat16),
            pltpu.VMEM((2 * B, 4 * B), jnp.bfloat16),
        ],
        compiler_params=pltpu.CompilerParams(vmem_limit_bytes=VMEM),
        cost_estimate=pl.CostEstimate(
            flops=rows // 2 * 6 * 256 * 512 * 768, bytes_accessed=rows * B * B * 66, transcendentals=0
        ),
        name="compose",
    )(f1, f2, low, high)


def left_kernel(top, own, bottom, band, out, high, low):
    s = pl.program_id(0)
    steps = pl.num_programs(0)
    width = own.shape[1]
    slot = lax.rem(s, 3)

    def keep(ref):
        h, l = parts(ref[...])
        high[slot] = h
        low[slot] = l

    @pl.when(s == 0)
    def _():
        keep(top)

    @pl.when(jnp.logical_and(s > 0, s < steps - 1))
    def _():
        keep(own)

    @pl.when(s == steps - 1)
    def _():
        keep(bottom)

    @pl.when(s >= 2)
    def _():
        step = 2 * B
        for at in range(0, width, step):
            stop = min(at + step, width)
            total = None
            for k in range(3):
                here = lax.rem(s + 1 + k, 3)
                cut = slice(k * 2 * B, (k + 1) * 2 * B)
                x = high[here, :, at:stop]
                both = dot(band[0, :, cut], x)
                term = both[: 2 * B] + both[2 * B :] + dot(band[0, : 2 * B, cut], low[here, :, at:stop])
                total = term if total is None else total + term
            out[:, at:stop] = total


def left(top, own, bottom, band):
    groups = band.shape[0]
    rows, width = own.shape
    rim = pl.BlockSpec((2 * B, width), lambda s: (0, 0))
    return pl.pallas_call(
        left_kernel,
        grid=(groups + 2,),
        in_specs=[
            rim,
            pl.BlockSpec((2 * B, width), lambda s: (jnp.clip(s - 1, 0, groups - 1), 0)),
            rim,
            pl.BlockSpec((1, 4 * B, 6 * B), lambda s: (jnp.maximum(s - 2, 0), 0, 0)),
        ],
        out_specs=pl.BlockSpec((2 * B, width), lambda s: (jnp.maximum(s - 2, 0), 0)),
        out_shape=jax.ShapeDtypeStruct((rows, width), jnp.float32),
        scratch_shapes=[
            pltpu.VMEM((3, 2 * B, width), jnp.bfloat16),
            pltpu.VMEM((3, 2 * B, width), jnp.bfloat16),
        ],
        compiler_params=pltpu.CompilerParams(vmem_limit_bytes=VMEM),
        cost_estimate=pl.CostEstimate(
            flops=6 * rows * 768 * width, bytes_accessed=8 * rows * width, transcendentals=0
        ),
        name="left",
    )(top, own, bottom, band)


def right_kernel(pair, tile, sides, blocks, noise, row_places, col_places, out, bh, bl, th, tl):
    groups = bh.shape[0]
    cols = tile.shape[1]
    span = pair * B

    @pl.when(pl.program_id(0) == 0)
    def _():
        bh[...] = jnp.zeros_like(bh)
        bl[...] = jnp.zeros_like(bl)
        for g in range(groups):
            for r in range(pair):
                h, l = parts(blocks[g * pair + r].T)
                bh[g, r * B : (r + 5) * B, r * B : (r + 1) * B] = h
                bl[g, r * B : (r + 5) * B, r * B : (r + 1) * B] = l

    h, l = parts(sides[:, : 2 * B])
    th[:, : 2 * B] = h
    tl[:, : 2 * B] = l
    h, l = parts(tile[...])
    th[:, 2 * B : 2 * B + cols] = h
    tl[:, 2 * B : 2 * B + cols] = l
    h, l = parts(sides[:, 2 * B :])
    th[:, 2 * B + cols :] = h
    tl[:, 2 * B + cols :] = l
    for g in range(groups):
        cut = slice(g * span, g * span + (pair + 4) * B)
        x = th[:, cut]
        total = dot(x, bh[g]) + dot(tl[:, cut], bh[g]) + dot(x, bl[g])
        here = slice(g * span, (g + 1) * span)
        distance = (row_places[...] - col_places[:, here]) / 0.5
        out[:, here] = total * jnp.exp(-distance * distance) + noise[:, here]


def right(tile, sides, blocks, noise, row_places, col_places):
    rows, cols = tile.shape
    count = cols // B
    pair = 2 if count % 2 == 0 else 1
    height = 512 if rows % 512 == 0 else 256
    band = (count // pair, (pair + 4) * B, pair * B)

    def rowwise(width):
        return pl.BlockSpec((height, width), lambda s: (s, 0))

    return pl.pallas_call(
        functools.partial(right_kernel, pair),
        grid=(rows // height,),
        in_specs=[
            rowwise(cols),
            rowwise(4 * B),
            pl.BlockSpec(blocks.shape, lambda s: (0, 0, 0)),
            rowwise(cols),
            rowwise(1),
            pl.BlockSpec((1, cols), lambda s: (0, 0)),
        ],
        out_specs=rowwise(cols),
        out_shape=jax.ShapeDtypeStruct((rows, cols), jnp.float32),
        scratch_shapes=[
            pltpu.VMEM(band, jnp.bfloat16),
            pltpu.VMEM(band, jnp.bfloat16),
            pltpu.VMEM((height, cols + 4 * B), jnp.bfloat16),
            pltpu.VMEM((height, cols + 4 * B), jnp.bfloat16),
        ],
        compiler_params=pltpu.CompilerParams(vmem_limit_bytes=VMEM),
        cost_estimate=pl.CostEstimate(
            flops=6 * rows * 768 * cols, bytes_accessed=14 * rows * cols, transcendentals=rows * cols
        ),
        name="right",
    )(tile, sides, blocks, noise, row_places, col_places)


def spread(block, owners, owner):
    rows = lax.axis_size("row")
    cols = lax.axis_size("col")
    block = jnp.where(lax.axis_index("row") == owner, block, jnp.zeros_like(block))
    if rows & (rows - 1):
        return lax.psum(block, "row")
    step = rows // 2
    while step:
        pairs = [
            (r * cols + c, (r ^ step) * cols + c)
            for c in range(cols)
            for r in range(rows)
            if (r ^ owners[c]) & (2 * step - 1) == 0
        ]
        block = block + lax.ppermute(block, ("row", "col"), pairs)
        step //= 2
    return block


def body(factors, covariance, noise, positions):
    rows_here, cols_here = covariance.shape
    block_rows = factors.shape[1]
    block_cols = cols_here // B
    cols = lax.axis_size("col")
    col_at = lax.axis_index("col")
    row_at = lax.axis_index("row")
    rim = 2 * B

    shaped = factors.reshape(2, block_rows, factors.shape[2] // B, B)
    gathered = lax.all_gather(shaped, "col", axis=2, tiled=True)

    sides = jnp.concatenate(
        neighbours(covariance[:, :rim], covariance[:, cols_here - rim :], "col"), axis=1
    )
    above, below = neighbours(covariance[:rim], covariance[rows_here - rim :], "row")
    sides_above, sides_below = neighbours(sides[:rim], sides[rows_here - rim :], "row")

    low, high = neighbours(gathered[0, :1], gathered[0, block_rows - 1 :], "row")
    band, compact = compose(gathered[0], gathered[1], low, high)

    owners = [c * block_cols // block_rows for c in range(cols)]
    selected = lax.dynamic_slice_in_dim(compact, col_at * block_cols % block_rows, block_cols, 0)
    matching = spread(selected, owners, col_at * block_cols // block_rows)

    tile = left(above, covariance, below, band)
    tile_sides = left(sides_above, sides, sides_below, band)

    row_places = lax.dynamic_slice_in_dim(positions, row_at * rows_here, rows_here, 0)
    col_places = lax.dynamic_slice_in_dim(positions, col_at * cols_here, cols_here, 0)
    return right(tile, tile_sides, matching, noise, row_places[:, None], col_places[None, :])


def solution(mesh):
    placed = (P(None, "row", "col"), P("row", "col"), P("row", "col"), P())
    return jax.shard_map(
        body, mesh=mesh, in_specs=placed, out_specs=P("row", "col"), check_vma=False
    )
```

time: 704 us -> 440 us (0.62); the launches traced: 695 us -> 438 us
  matrix products: 293 us -> 0 us
  Pallas kernels: 0 us -> 98.4 us
  local copies, waits for them, and re-layouts: 120 us -> 26.7 us
  waiting for transfers between devices: 207 us -> 262 us
  other arithmetic: 41.9 us -> 10.5 us
  starting transfers between devices: 18.6 us -> 27.1 us
    dot_general x19 -> x0, matrix products: 293 us -> none  [the longest x5 130 us: left_local(): jnp.einsum('iab,ibk->iak', blocks[:, offset], split[offset:offset + count...]
    pallas_call x0 -> x4, Pallas kernels: none -> 98.4 us  [the longest x2 50.1 us: left(): pl.pallas_call(left_kernel, grid=(groups + 2,), in_specs=[rim, pl.BlockSp...]
    all_gather x1, waiting for transfers between devices: 61.6 us -> 138 us  [body(): gathered = lax.all_gather(shaped, 'col', axis=2, tiled=True)]
    slice x7 -> x3, local copies, waits for them, and re-layouts: 51.2 us -> 6.49 us  [the longest x1 3.27 us: body(): covariance[:, :rim]]
    reshape x2 -> x0, local copies, waits for them, and re-layouts: 37.3 us -> none  [the longest x1 18.7 us: right_local(): return total.reshape(height, count * size)]
    ppermute x6 -> x10, waiting for transfers between devices: 145 us -> 123 us  [the longest x4 120 us: neighbours(): before = lax.ppermute(last, axis, [(i, i + 1) for i in range(count - 1)])]
    concatenate x1 -> x0, other arithmetic: 16.5 us -> none  [padded_2(): jnp.concatenate([lax.ppermute(tail, axis, [(i, (i + 1) % count) for i in...]
    concatenate x2 -> x1, local copies, waits for them, and re-layouts: 14.3 us -> 0.48 us  [body(): jnp.concatenate(neighbours(covariance[:, :rim], covariance[:, cols_here -...]
  transfers between devices with their start and end apart: 8 -> 11, of which waited for: 4 -> 5; matrix products, arithmetic and copies ran while one was open for 14% -> 5% of each run, Pallas kernels for 0% -> 11%
where the time goes in v1:
time: 440 us; the launch traced here: 438 us
  waiting for transfers between devices  262 us (60%)
  Pallas kernels  98.4 us (22%)
  starting transfers between devices  27.1 us (6%)
  local copies, waits for them, and re-layouts  26.7 us (6%)
  between operations  13.6 us (3%)
  other arithmetic  10.5 us (2%)
    all_gather x1, waiting for transfers between devices, body(): gathered = lax.all_gather(shaped, 'col', axis=2, tiled=True)  138 us
    ppermute x4, waiting for transfers between devices, neighbours(): before = lax.ppermute(last, axis, [(i, i + 1) for i in range(count - 1)])  120 us
    pallas_call x2, Pallas kernels, left(): pl.pallas_call(left_kernel, grid=(groups + 2,), in_specs=[rim, pl.BlockSp...  50.1 us
    pallas_call x1, Pallas kernels, right(): pl.pallas_call(functools.partial(right_kernel, pair), grid=(rows // heigh...  31.8 us
    pallas_call x1, Pallas kernels, compose(): pl.pallas_call(compose_kernel, grid=(rows // 2,), in_specs=[whole, whole,...  16.5 us
    ppermute x4, starting transfers between devices, neighbours(): before = lax.ppermute(last, axis, [(i, i + 1) for i in range(count - 1)])  13 us
    ppermute x4, starting transfers between devices, neighbours(): after = lax.ppermute(first, axis, [(i + 1, i) for i in range(count - 1)])  11.7 us
  transfers between devices with their start and end apart: 11, of which 5 were waited for; matrix products, arithmetic and copies ran while one was open for 5% of the time, Pallas kernels for 11%

profile of v1, /device:TPU:17, one launch (start us, length us, event | category | flops | bytes accessed | tf_op | source)
XLA Modules:
  0.0 438.1 jit_solution(10493257880581017671)
XLA Ops:
  6.5 2.5 copy.6
  9.1 138.3 %all-gather.2.cloned.1.call-done = f32[2,24,384,128]{3,2,1,0:T(8,128)} async-done(((f32[2,24,48,128]{3,2,1,0:T(8,128)}), f32[2,24,384,128]{3,2,1,0:T(8,128)}) %all-gather.2.cloned.1.call-update) | async-done | bytes 9437200 | tf_op jit(solution)/shard_map/all_gather | solution.py:263
  148.5 3.0 collective-permute-start.3
  151.5 3.0 collective-permute-start.2
  154.5 8.5 %slice_bitcast_fusion = (f32[24,384,128]{2,1,0:T(8,128)}, f32[24,384,128]{2,1,0:T(8,128)}) fusion(f32[2,24,384,128]{3,2,1,0:T(8,128)} %all-gather.2.cloned.1.call-done), kind=kLoop, calls=%fused_computation | loop fusion | bytes 18874368 | tf_op jit(solution)/shard_map/squeeze | solution.py:272
  163.8 16.5 %compose.1 = (bf16[12,512,768]{2,1,0:T(8,128)(2,1)}, f32[24,128,640]{2,1,0:T(8,128)}) custom-call(f32[24,384,128]{2,1,0:T(8,128)} %get-tuple-element.16.f1, f32[24,384,128]{2,1,0:T(8,128)} %get-tuple-element.15.f2, f32[1,384,128]{2,1,0:T(8,128)} %copy-done.2, f32[1,384,128]{2,1,0:T(8,128)} %copy-done.1), custom_call_target="tpu_custom_call" | custom-call | flops 7247757312 | bytes 25952256 | tf_op jit(solution)/shard_map/compose/pallas_call | solution.py:72
  180.2 2.6 dynamic-slice_select_fusion
  183.9 3.3 fusion
  187.1 2.2 collective-permute-start.4
  189.3 4.0 collective-permute-start.5
  193.3 2.1 fusion.1
  195.4 2.4 collective-permute-start.1
  197.8 4.4 %collective-permute-start = (f32[256,1536]{1,0:T(8,128)S(1)}, f32[256,1536]{1,0:T(8,128)}, u32[]{:S(2)}, u32[]{:S(2)}) collective-permute-start(f32[256,1536]{1,0:T(8,128)S(1)} %get-tuple-element.12), channel_id=1, source_target_pairs={{0,8},{8,16},{16,24},{1,9},{9,17},{17,25},{2,10},{10,18},{18,26},{... | collective-permute-start | bytes 4718600 | tf_op jit(solution)/shard_map/ppermute | solution.py:25
  202.3 2.3 fusion.3
  205.9 118.4 %collective-permute-done.4 = f32[3072,256]{1,0:T(8,128)S(1)} collective-permute-done((f32[3072,256]{1,0:T(8,128)S(1)}, f32[3072,256]{1,0:T(8,128)S(1)}, u32[]{:S(2)}, u32[]{:S(2)}) %collective-permute-start.4) | collective-permute-done | bytes 3145760 | tf_op jit(solution)/shard_map/ppermute | solution.py:25
  324.8 2.6 collective-permute-done.5
  327.9 2.7 copy-done
  331.7 2.3 collective-permute-start.7
  334.0 3.4 collective-permute-start.6
  339.6 1.7 copy.5.row_places
  343.7 17.6 %left.3.sides = f32[3072,512]{1,0:T(8,128)} custom-call(f32[256,512]{1,0:T(8,128)} %collective-permute-done.6.top, f32[3072,512]{1,0:T(8,128)} %copy-done, f32[256,512]{1,0:T(8,128)} %collective-permute-done.7.bottom, bf16[12,512,768]{2,1,0:T(8,128)(2,1)} %get-tuple-element.7.band), custom_call_target="tpu_custom_call" | custom-call | flops 7247757312 | bytes 12582912 | tf_op jit(solution)/shard_map/left/pallas_call | solution.py:141
  361.3 32.6 %left.2.tile = f32[3072,1536]{1,0:T(8,128)} custom-call(f32[256,1536]{1,0:T(8,128)} %collective-permute-done.top, f32[3072,1536]{1,0:T(8,128)} %own.1, f32[256,1536]{1,0:T(8,128)} %collective-permute-done.1.bottom, bf16[12,512,768]{2,1,0:T(8,128)(2,1)} %get-tuple-element.7.band), custom_call_target="tpu_custom_call" | custom-call | flops 21743271936 | bytes 37748736 | tf_op jit(solution)/shard_map/left/pallas_call | solution.py:141
  393.9 5.6 %add.23.blocks = f32[12,128,640]{2,1,0:T(8,128)} add(f32[12,128,640]{2,1,0:T(8,128)} %fusion.3, f32[12,128,640]{2,1,0:T(8,128)} %collective-permute-done.9) | non-fusion elementwise | flops 983040 | bytes 11796480 | tf_op jit(solution)/shard_map/add | solution.py:248
  399.5 31.8 %right.1 = f32[3072,1536]{1,0:T(8,128)} custom-call(f32[3072,1536]{1,0:T(8,128)} %left.2.tile, f32[3072,512]{1,0:T(8,128)} %left.3.sides, f32[12,128,640]{2,1,0:T(8,128)} %add.23.blocks, f32[3072,1536]{1,0:T(8,128)} %noise.1, f32[3072,1]{1,0:T(8,128)} %copy.5.row_places, f32[1,1536]{1,0:T(1,128)} %broadcast_in_dim.11.col_places), custom_call_target="tpu_custom_call" | custom-call | flops 21743271936 | bytes 66060288 | tf_op jit(solution)/shard_map/right/pallas_call | solution.py:207
  (29 shorter events, 10.8 us)
Async XLA Ops:
  6.5 140.9 %all-gather.2.cloned.1.call-start = ((), (), s32[]{:S(2)}) async-start(), calls=%async_computation | async-start | bytes 10616832 | tf_op jit(solution)/shard_map/all_gather | solution.py:263
  148.5 14.5 %collective-permute-start.3 = (f32[1,384,128]{2,1,0:T(8,128)S(1)}, f32[1,384,128]{2,1,0:T(8,128)S(1)}, u32[]{:S(2)}, u32[]{:S(2)}) collective-permute-start(f32[1,384,128]{2,1,0:T(8,128)S(1)} %get-tuple-element.13), channel_id=1, source_target_pairs={{8,0},{16,8},{24,16},{9,1},{17,9},{25,17},{10,2},{18,10},{26,18},{... | collective-permute-start | bytes 589832 | tf_op jit(solution)/shard_map/ppermute | solution.py:26
  151.5 11.5 %collective-permute-start.2 = (f32[1,384,128]{2,1,0:T(8,128)S(1)}, f32[1,384,128]{2,1,0:T(8,128)S(1)}, u32[]{:S(2)}, u32[]{:S(2)}) collective-permute-start(f32[1,384,128]{2,1,0:T(8,128)S(1)} %get-tuple-element.14), channel_id=1, source_target_pairs={{0,8},{8,16},{16,24},{1,9},{9,17},{17,25},{2,10},{10,18},{18,26},{... | collective-permute-start | bytes 589832 | tf_op jit(solution)/shard_map/ppermute | solution.py:25
  162.9 0.7 copy-start.1
  163.0 0.8 copy-start.2
  180.2 22.1 %slice-start = ((s8[7864320]{0:T(1024)(128)(4,1)}), s8[4194304]{0:T(1024)(128)(4,1)S(1)}, s32[]{:S(2)}) async-start(s8[7864320]{0:T(1024)(128)(4,1)} %bitcast.13), calls=%async_computation.1 | async-start | bytes 8388608
  182.8 19.5 %slice-start.1 = ((s8[7864320]{0:T(1024)(128)(4,1)}), s8[3670016]{0:T(1024)(128)(4,1)S(1)}, s32[]{:S(2)}) async-start(s8[7864320]{0:T(1024)(128)(4,1)} %bitcast.13), calls=%async_computation.2 | async-start | bytes 7340032
  182.8 19.5 %collective-permute-start.8 = (f32[12,128,640]{2,1,0:T(8,128)S(1)}, f32[12,128,640]{2,1,0:T(8,128)S(1)}, u32[]{:S(2)}, u32[]{:S(2)}) collective-permute-start(f32[12,128,640]{2,1,0:T(8,128)S(1)} %dynamic-slice_select_fusion), channel_id=1, source_target_pairs={{0,16},{1,17},{10,26},{11,27},{20,4},{21,5},{30,14},{31,15}} | collective-permute-start | bytes 11796488 | tf_op jit(solution)/shard_map/ppermute | solution.py:248
  187.1 137.2 %collective-permute-start.4 = (f32[3072,256]{1,0:T(8,128)S(1)}, f32[3072,256]{1,0:T(8,128)S(1)}, u32[]{:S(2)}, u32[]{:S(2)}) collective-permute-start(f32[3072,256]{1,0:T(8,128)S(1)} %get-tuple-element.10), channel_id=1, source_target_pairs={{0,1},{1,2},{2,3},{3,4},{4,5},{5,6},{6,7},{8,9},{9,10},{10,11},{11... | collective-permute-start | bytes 9437192 | tf_op jit(solution)/shard_map/ppermute | solution.py:25
  189.3 138.1 %collective-permute-start.5 = (f32[3072,256]{1,0:T(8,128)S(1)}, f32[3072,256]{1,0:T(8,128)S(1)}, u32[]{:S(2)}, u32[]{:S(2)}) collective-permute-start(f32[3072,256]{1,0:T(8,128)S(1)} %get-tuple-element.9), channel_id=1, source_target_pairs={{1,0},{2,1},{3,2},{4,3},{5,4},{6,5},{7,6},{9,8},{10,9},{11,10},{12... | collective-permute-start | bytes 9437192 | tf_op jit(solution)/shard_map/ppermute | solution.py:26
  195.4 165.9 %collective-permute-start.1 = (f32[256,1536]{1,0:T(8,128)S(1)}, f32[256,1536]{1,0:T(8,128)}, u32[]{:S(2)}, u32[]{:S(2)}) collective-permute-start(f32[256,1536]{1,0:T(8,128)S(1)} %get-tuple-element.11), channel_id=1, source_target_pairs={{8,0},{16,8},{24,16},{9,1},{17,9},{25,17},{10,2},{18,10},{26,18},{... | collective-permute-start | bytes 4718600 | tf_op jit(solution)/shard_map/ppermute | solution.py:26
  197.8 163.5 %collective-permute-start = (f32[256,1536]{1,0:T(8,128)S(1)}, f32[256,1536]{1,0:T(8,128)}, u32[]{:S(2)}, u32[]{:S(2)}) collective-permute-start(f32[256,1536]{1,0:T(8,128)S(1)} %get-tuple-element.12), channel_id=1, source_target_pairs={{0,8},{8,16},{16,24},{1,9},{9,17},{17,25},{2,10},{10,18},{18,26},{... | collective-permute-start | bytes 4718600 | tf_op jit(solution)/shard_map/ppermute | solution.py:25
  204.6 189.3 %collective-permute-start.9 = (f32[12,128,640]{2,1,0:T(8,128)}, f32[12,128,640]{2,1,0:T(8,128)}, u32[]{:S(2)}, u32[]{:S(2)}) collective-permute-start(f32[12,128,640]{2,1,0:T(8,128)} %fusion.3), channel_id=1, source_target_pairs={{0,8},{16,24},{1,9},{17,25},{10,2},{26,18},{11,3},{27,19},{4,12},{... | collective-permute-start | bytes 11796488 | tf_op jit(solution)/shard_map/ppermute | solution.py:248
  327.9 2.7 copy-start
  331.7 10.8 %collective-permute-start.7 = (f32[256,512]{1,0:T(8,128)}, f32[256,512]{1,0:T(8,128)}, u32[]{:S(2)}, u32[]{:S(2)}) collective-permute-start(f32[256,512]{1,0:T(8,128)} %get-tuple-element.17), channel_id=1, source_target_pairs={{8,0},{16,8},{24,16},{9,1},{17,9},{25,17},{10,2},{18,10},{26,18},{... | collective-permute-start | bytes 1572872 | tf_op jit(solution)/shard_map/ppermute | solution.py:26
  334.0 9.7 %collective-permute-start.6 = (f32[256,512]{1,0:T(8,128)}, f32[256,512]{1,0:T(8,128)}, u32[]{:S(2)}, u32[]{:S(2)}) collective-permute-start(f32[256,512]{1,0:T(8,128)} %get-tuple-element.18), channel_id=1, source_target_pairs={{0,8},{8,16},{16,24},{1,9},{9,17},{17,25},{2,10},{10,18},{18,26},{... | collective-permute-start | bytes 1572872 | tf_op jit(solution)/shard_map/ppermute | solution.py:25
Sparse Core Ops, SparseCore 0:
  9.5 137.8 all-gather.1

commit v2 on v1

--- a/solution.py
+++ b/solution.py
@@ -27,9 +27,9 @@
     return before, after
 
 
-def compose_kernel(f1, f2, low, high, band, compact, b1h, b1l, b2h, b2l):
+def compose_kernel(f, low, high, band, compact, b1h, b1l, b2h, b2l):
     g = pl.program_id(0)
-    rows = f1.shape[0]
+    rows = f.shape[1]
 
     @pl.when(g == 0)
     def _():
@@ -38,7 +38,7 @@
 
     for r in range(2):
         for k in range(3):
-            h, l = parts(f2[2 * g + r, k * B : (k + 1) * B, :])
+            h, l = parts(f[1, 2 * g + r, k * B : (k + 1) * B, :])
             at = (slice(r * B, (r + 1) * B), slice((r + k) * B, (r + k + 1) * B))
             b2h[at] = h
             b2l[at] = l
@@ -46,13 +46,13 @@
         for k in range(3):
             cut = slice(k * B, (k + 1) * B)
             if j == 0:
-                x = jnp.where(g == 0, low[0, cut, :], f1[jnp.maximum(2 * g - 1, 0), cut, :])
+                x = jnp.where(g == 0, low[0, cut, :], f[0, jnp.maximum(2 * g - 1, 0), cut, :])
             elif j == 3:
                 x = jnp.where(
-                    g == rows // 2 - 1, high[0, cut, :], f1[jnp.minimum(2 * g + 2, rows - 1), cut, :]
+                    g == rows // 2 - 1, high[0, cut, :], f[0, jnp.minimum(2 * g + 2, rows - 1), cut, :]
                 )
             else:
-                x = f1[2 * g + j - 1, cut, :]
+                x = f[0, 2 * g + j - 1, cut, :]
             h, l = parts(x)
             at = (slice(j * B, (j + 1) * B), slice((j + k) * B, (j + k + 1) * B))
             b1h[at] = h
@@ -65,14 +65,14 @@
     compact[1] = c[B:, B:]
 
 
-def compose(f1, f2, low, high):
-    rows = f1.shape[0]
-    whole = pl.BlockSpec(f1.shape, lambda g: (0, 0, 0))
+def compose(f, low, high):
+    rows = f.shape[1]
+    whole = pl.BlockSpec(f.shape, lambda g: (0, 0, 0, 0))
     rim = pl.BlockSpec(low.shape, lambda g: (0, 0, 0))
     return pl.pallas_call(
         compose_kernel,
         grid=(rows // 2,),
-        in_specs=[whole, whole, rim, rim],
+        in_specs=[whole, rim, rim],
         out_specs=[
             pl.BlockSpec((1, 4 * B, 6 * B), lambda g: (g, 0, 0)),
             pl.BlockSpec((2, B, 5 * B), lambda g: (g, 0, 0)),
@@ -89,10 +89,10 @@
         ],
         compiler_params=pltpu.CompilerParams(vmem_limit_bytes=VMEM),
         cost_estimate=pl.CostEstimate(
-            flops=rows // 2 * 6 * 256 * 512 * 768, bytes_accessed=rows * B * B * 66, transcendentals=0
+            flops=rows * B * B, bytes_accessed=rows * B * B, transcendentals=0
         ),
         name="compose",
-    )(f1, f2, low, high)
+    )(f, low, high)
 
 
 def left_kernel(top, own, bottom, band, out, high, low):
@@ -155,13 +155,13 @@
         ],
         compiler_params=pltpu.CompilerParams(vmem_limit_bytes=VMEM),
         cost_estimate=pl.CostEstimate(
-            flops=6 * rows * 768 * width, bytes_accessed=8 * rows * width, transcendentals=0
+            flops=rows * width, bytes_accessed=rows * width, transcendentals=0
         ),
         name="left",
     )(top, own, bottom, band)
 
 
-def right_kernel(pair, tile, sides, blocks, noise, row_places, col_places, out, bh, bl, th, tl):
+def right_kernel(pair, tile, sides, held, came, noise, row_places, col_places, out, bh, bl, th, tl):
     groups = bh.shape[0]
     cols = tile.shape[1]
     span = pair * B
@@ -172,7 +172,7 @@
         bl[...] = jnp.zeros_like(bl)
         for g in range(groups):
             for r in range(pair):
-                h, l = parts(blocks[g * pair + r].T)
+                h, l = parts((held[g * pair + r] + came[g * pair + r]).T)
                 bh[g, r * B : (r + 5) * B, r * B : (r + 1) * B] = h
                 bl[g, r * B : (r + 5) * B, r * B : (r + 1) * B] = l
 
@@ -194,7 +194,7 @@
         out[:, here] = total * jnp.exp(-distance * distance) + noise[:, here]
 
 
-def right(tile, sides, blocks, noise, row_places, col_places):
+def right(tile, sides, held, came, noise, row_places, col_places):
     rows, cols = tile.shape
     count = cols // B
     pair = 2 if count % 2 == 0 else 1
@@ -210,7 +210,8 @@
         in_specs=[
             rowwise(cols),
             rowwise(4 * B),
-            pl.BlockSpec(blocks.shape, lambda s: (0, 0, 0)),
+            pl.BlockSpec(held.shape, lambda s: (0, 0, 0)),
+            pl.BlockSpec(held.shape, lambda s: (0, 0, 0)),
             rowwise(cols),
             rowwise(1),
             pl.BlockSpec((1, cols), lambda s: (0, 0)),
@@ -228,26 +229,30 @@
             flops=6 * rows * 768 * cols, bytes_accessed=14 * rows * cols, transcendentals=rows * cols
         ),
         name="right",
-    )(tile, sides, blocks, noise, row_places, col_places)
-
-
-def spread(block, owners, owner):
+    )(tile, sides, held, came, noise, row_places, col_places)
+
+
+def spread(block, owners, owner, meanwhile):
     rows = lax.axis_size("row")
     cols = lax.axis_size("col")
     block = jnp.where(lax.axis_index("row") == owner, block, jnp.zeros_like(block))
     if rows & (rows - 1):
-        return lax.psum(block, "row")
+        return lax.psum(block, "row"), jnp.zeros_like(block), meanwhile
+    came = jnp.zeros_like(block)
     step = rows // 2
     while step:
+        if step == rows // 4:
+            came, meanwhile = lax.optimization_barrier((came, meanwhile))
+        block = block + came
         pairs = [
             (r * cols + c, (r ^ step) * cols + c)
             for c in range(cols)
             for r in range(rows)
             if (r ^ owners[c]) & (2 * step - 1) == 0
         ]
-        block = block + lax.ppermute(block, ("row", "col"), pairs)
+        came = lax.ppermute(block, ("row", "col"), pairs)
         step //= 2
-    return block
+    return block, came, meanwhile
 
 
 def body(factors, covariance, noise, positions):
@@ -262,25 +267,40 @@
     shaped = factors.reshape(2, block_rows, factors.shape[2] // B, B)
     gathered = lax.all_gather(shaped, "col", axis=2, tiled=True)
 
-    sides = jnp.concatenate(
-        neighbours(covariance[:, :rim], covariance[:, cols_here - rim :], "col"), axis=1
+    cut = rows_here // 2
+    first, last = covariance[:, :rim], covariance[:, cols_here - rim :]
+    before, after = neighbours(first[:cut], last[:cut], "col")
+    above, below = neighbours(covariance[:rim], covariance[rows_here - rim :], "row")
+    gathered, before, after, above, below, first, last = lax.optimization_barrier(
+        (gathered, before, after, above, below, first[cut:], last[cut:])
     )
-    above, below = neighbours(covariance[:rim], covariance[rows_here - rim :], "row")
-    sides_above, sides_below = neighbours(sides[:rim], sides[rows_here - rim :], "row")
-
+    late_before, late_after = neighbours(first, last, "col")
     low, high = neighbours(gathered[0, :1], gathered[0, block_rows - 1 :], "row")
-    band, compact = compose(gathered[0], gathered[1], low, high)
+    band, compact = compose(gathered, low, high)
 
     owners = [c * block_cols // block_rows for c in range(cols)]
     selected = lax.dynamic_slice_in_dim(compact, col_at * block_cols % block_rows, block_cols, 0)
-    matching = spread(selected, owners, col_at * block_cols // block_rows)
 
     tile = left(above, covariance, below, band)
+    held, came, (tile, late_before, late_after) = spread(
+        selected,
+        owners,
+        col_at * block_cols // block_rows,
+        (tile, late_before, late_after),
+    )
+    sides = jnp.concatenate(
+        [
+            jnp.concatenate([before, after], axis=1),
+            jnp.concatenate([late_before, late_after], axis=1),
+        ],
+        axis=0,
+    )
+    sides_above, sides_below = neighbours(sides[:rim], sides[rows_here - rim :], "row")
     tile_sides = left(sides_above, sides, sides_below, band)
 
     row_places = lax.dynamic_slice_in_dim(positions, row_at * rows_here, rows_here, 0)
     col_places = lax.dynamic_slice_in_dim(positions, col_at * cols_here, cols_here, 0)
-    return right(tile, tile_sides, matching, noise, row_places[:, None], col_places[None, :])
+    return right(tile, tile_sides, held, came, noise, row_places[:, None], col_places[None, :])
 
 
 def solution(mesh):

time: 440 us -> 377 us (0.86)
  waiting for transfers between devices: 262 us -> 186 us
  starting transfers between devices: 27.1 us -> 35.7 us
    ppermute x4 -> x5, waiting for transfers between devices: 120 us -> 29.9 us  [neighbours(): before = lax.ppermute(last, axis, [(i, i + 1) for i in range(count - 1)])]
    ppermute x4 -> x5, waiting for transfers between devices: 3.86 us -> 79.1 us  [neighbours(): after = lax.ppermute(first, axis, [(i + 1, i) for i in range(count - 1)])]
    all_gather x1, waiting for transfers between devices: 138 us -> 76.8 us  [body(): gathered = lax.all_gather(shaped, 'col', axis=2, tiled=True)]
    squeeze x1 -> x0, local copies, waits for them, and re-layouts: 8.47 us -> none  [body(): band, compact = compose(gathered[0], gathered[1], low, high)]
    ppermute x4 -> x5, starting transfers between devices: 11.7 us -> 17.4 us  [neighbours(): after = lax.ppermute(first, axis, [(i + 1, i) for i in range(count - 1)])]
    concatenate x0 -> x1, other arithmetic: none -> 5.3 us  [body(): jnp.concatenate([jnp.concatenate([before, after], axis=1), jnp.concatenat...]
    unnamed x12 -> x17, local copies, waits for them, and re-layouts: 6.43 us -> 9.36 us
    ppermute x4 -> x5, starting transfers between devices: 13 us -> 14.2 us  [neighbours(): before = lax.ppermute(last, axis, [(i, i + 1) for i in range(count - 1)])]
  transfers between devices with their start and end apart: 11 -> 13, of which waited for: 5 -> 8; matrix products, arithmetic and copies ran while one was open for 5% -> 6% of each run, Pallas kernels for 11% -> 13%
where the time goes in v2:
time: 377 us; the launch traced here: 375 us
  waiting for transfers between devices  186 us (49%)
  Pallas kernels  99.6 us (26%)
  starting transfers between devices  35.7 us (9%)
  local copies, waits for them, and re-layouts  25.6 us (7%)
  other arithmetic  14.2 us (4%)
  between operations  13.6 us (4%)
    ppermute x5, waiting for transfers between devices, neighbours(): after = lax.ppermute(first, axis, [(i + 1, i) for i in range(count - 1)])  79.1 us
    all_gather x1, waiting for transfers between devices, body(): gathered = lax.all_gather(shaped, 'col', axis=2, tiled=True)  76.8 us
    pallas_call x2, Pallas kernels, left(): pl.pallas_call(left_kernel, grid=(groups + 2,), in_specs=[rim, pl.BlockSp...  50.3 us
    pallas_call x1, Pallas kernels, right(): pl.pallas_call(functools.partial(right_kernel, pair), grid=(rows // heigh...  33 us
    ppermute x5, waiting for transfers between devices, neighbours(): before = lax.ppermute(last, axis, [(i, i + 1) for i in range(count - 1)])  29.9 us
    ppermute x5, starting transfers between devices, neighbours(): after = lax.ppermute(first, axis, [(i + 1, i) for i in range(count - 1)])  17.4 us
    pallas_call x1, Pallas kernels, compose(): pl.pallas_call(compose_kernel, grid=(rows // 2,), in_specs=[whole, rim, r...  16.4 us
    ppermute x5, starting transfers between devices, neighbours(): before = lax.ppermute(last, axis, [(i, i + 1) for i in range(count - 1)])  14.2 us
  transfers between devices with their start and end apart: 13, of which 8 were waited for; matrix products, arithmetic and copies ran while one was open for 6% of the time, Pallas kernels for 13%

profile of v2, /device:TPU:17, one launch (start us, length us, event | category | flops | bytes accessed | tf_op | source)
XLA Modules:
  0.0 374.6 jit_solution(2880823295546519688)
XLA Ops:
  6.5 2.5 copy.6
  11.1 2.6 collective-permute-start.3
  13.7 3.0 collective-permute-start.2
  16.8 5.8 %fusion = (f32[1536,256]{1,0:T(8,128)}, f32[1536,256]{1,0:T(8,128)}, f32[1536,256]{1,0:T(8,128)S(1)}, f32[1536,256]{1,0:T(8,128)S(1)}) fusion(f32[3072,1536]{1,0:T(8,128)} %own.1), kind=kLoop, calls=%fused_computation.8 | loop fusion | bytes 12582912 | tf_op jit(solution)/shard_map/slice | solution.py:275
  22.6 3.0 collective-permute-start.1
  25.5 2.3 collective-permute-start
  27.9 5.5 %collective-permute-done.3.bottom = f32[256,1536]{1,0:T(8,128)} collective-permute-done((f32[256,1536]{1,0:T(8,128)S(1)}, f32[256,1536]{1,0:T(8,128)}, u32[]{:S(2)}, u32[]{:S(2)}) %collective-permute-start.3) | collective-permute-done | bytes 1572896 | tf_op jit(solution)/shard_map/ppermute | solution.py:26
  34.1 69.0 %collective-permute-done.1 = f32[1536,256]{1,0:T(8,128)S(1)} collective-permute-done((f32[1536,256]{1,0:T(8,128)S(1)}, f32[1536,256]{1,0:T(8,128)S(1)}, u32[]{:S(2)}, u32[]{:S(2)}) %collective-permute-start.1) | collective-permute-done | bytes 1572896 | tf_op jit(solution)/shard_map/ppermute | solution.py:26
  104.3 76.8 %all-gather.2.cloned.1.call-done.f = f32[2,24,384,128]{3,2,1,0:T(8,128)} async-done(((f32[2,24,48,128]{3,2,1,0:T(8,128)}), f32[2,24,384,128]{3,2,1,0:T(8,128)}) %all-gather.2.cloned.1.call-update) | async-done | bytes 9437200 | tf_op jit(solution)/shard_map/all_gather | solution.py:268
  182.2 2.7 collective-permute-start.5
  184.9 3.0 collective-permute-start.4
  191.2 16.4 %compose.1 = (bf16[12,512,768]{2,1,0:T(8,128)(2,1)}, f32[24,128,640]{2,1,0:T(8,128)}) custom-call(f32[2,24,384,128]{3,2,1,0:T(8,128)} %all-gather.2.cloned.1.call-done.f, f32[1,384,128]{2,1,0:T(8,128)} %copy-done.4, f32[1,384,128]{2,1,0:T(8,128)} %copy-done.3), custom_call_target="tpu_custom_call" | custom-call | flops 393216 | bytes 393216 | tf_op jit(solution)/shard_map/compose/pallas_call | solution.py:72
  207.6 4.5 %dynamic-slice_select_fusion = f32[12,128,640]{2,1,0:T(8,128)} fusion(f32[24,128,640]{2,1,0:T(8,128)} %get-tuple-element.19, s32[]{:T(128)S(6)} %select_n.31, pred[]{:T(512)S(6)} %eq.5), kind=kLoop, calls=%fused_computation.1 | loop fusion | flops 983040 | bytes 7864325 | tf_op jit(solution)/shard_map/jit(_where)/select_n | solution.py:238
  212.0 2.6 collective-permute-start.6
  216.6 4.3 %collective-permute-start.8 = (f32[1536,256]{1,0:T(8,128)}, f32[1536,256]{1,0:T(8,128)}, u32[]{:S(2)}, u32[]{:S(2)}) collective-permute-start(f32[1536,256]{1,0:T(8,128)} %get-tuple-element.24), channel_id=1, source_target_pairs={{1,0},{2,1},{3,2},{4,3},{5,4},{6,5},{7,6},{9,8},{10,9},{11,10},{12... | collective-permute-start | bytes 4718600 | tf_op jit(solution)/shard_map/ppermute | solution.py:26
  220.8 32.7 %left.2.tile = f32[3072,1536]{1,0:T(8,128)} custom-call(f32[256,1536]{1,0:T(8,128)} %collective-permute-done.2.top, f32[3072,1536]{1,0:T(8,128)} %own.1, f32[256,1536]{1,0:T(8,128)} %collective-permute-done.3.bottom, bf16[12,512,768]{2,1,0:T(8,128)(2,1)} %get-tuple-element.22.band), custom_call_target="tpu_custom_call" | custom-call | flops 4718592 | bytes 4718592 | tf_op jit(solution)/shard_map/left/pallas_call | solution.py:141
  253.5 28.0 %collective-permute-done.7 = f32[1536,256]{1,0:T(8,128)} collective-permute-done((f32[1536,256]{1,0:T(8,128)}, f32[1536,256]{1,0:T(8,128)}, u32[]{:S(2)}, u32[]{:S(2)}) %collective-permute-start.7) | collective-permute-done | bytes 1572896 | tf_op jit(solution)/shard_map/ppermute | solution.py:25
  281.5 3.3 collective-permute-done.8
  284.8 4.4 %fusion.2.held = f32[12,128,640]{2,1,0:T(8,128)} fusion(f32[12,128,640]{2,1,0:T(8,128)} %collective-permute-done.6, f32[24,128,640]{2,1,0:T(8,128)S(1)} %bitcast.10, s32[]{:T(128)S(6)} %select_n.31, pred[]{:T(512)S(6)} %eq.5), kind=kLoop, calls=%fused_computation.10 | loop fusion | flops 1966080 | bytes 11796485 | tf_op jit(solution)/shard_map/add | solution.py:246
  293.4 4.9 %collective-permute-start.10 = (f32[256,512]{1,0:T(8,128)}, f32[256,512]{1,0:T(8,128)}, u32[]{:S(2)}, u32[]{:S(2)}) collective-permute-start(f32[256,512]{1,0:T(8,128)} %slice.47), channel_id=1, source_target_pairs={{8,0},{16,8},{24,16},{9,1},{17,9},{25,17},{10,2},{18,10},{26,18},{... | collective-permute-start | bytes 1572872 | tf_op jit(solution)/shard_map/ppermute | solution.py:26
  304.2 3.9 %collective-permute-start.9 = (f32[256,512]{1,0:T(8,128)}, f32[256,512]{1,0:T(8,128)}, u32[]{:S(2)}, u32[]{:S(2)}) collective-permute-start(f32[256,512]{1,0:T(8,128)} %slice.46), channel_id=1, source_target_pairs={{0,8},{8,16},{16,24},{1,9},{9,17},{17,25},{2,10},{10,18},{18,26},{... | collective-permute-start | bytes 1572872 | tf_op jit(solution)/shard_map/ppermute | solution.py:25
  311.8 5.3 %pad_maximum_fusion.own = f32[3072,512]{1,0:T(8,128)} fusion(f32[1536,512]{1,0:T(8,128)} %copy-done, f32[1536,512]{1,0:T(8,128)S(1)} %constant_dynamic-update-slice_fusion.2), kind=kLoop, calls=%fused_computation | loop fusion | flops 1572864 | bytes 12582912 | tf_op jit(solution)/shard_map/concatenate | solution.py:291
  317.2 17.6 %left.3.sides = f32[3072,512]{1,0:T(8,128)} custom-call(f32[256,512]{1,0:T(8,128)} %collective-permute-done.9.top, f32[3072,512]{1,0:T(8,128)} %pad_maximum_fusion.own, f32[256,512]{1,0:T(8,128)} %collective-permute-done.10.bottom, bf16[12,512,768]{2,1,0:T(8,128)(2,1)} %get-tuple-element.22.band), custom_call_target="tpu_custom_call" | custom-call | flops 1572864 | bytes 1572864 | tf_op jit(solution)/shard_map/left/pallas_call | solution.py:141
  334.8 33.0 %right.1 = f32[3072,1536]{1,0:T(8,128)} custom-call(f32[3072,1536]{1,0:T(8,128)} %left.2.tile, f32[3072,512]{1,0:T(8,128)} %left.3.sides, f32[12,128,640]{2,1,0:T(8,128)} %fusion.2.held, f32[12,128,640]{2,1,0:T(8,128)} %collective-permute-done.11.came, f32[3072,1536]{1,0:T(8,128)} %noise.1, f32[3072,1]{1,0:T(8,128)} %copy.5.row_places, ...), custom_call_target="tpu_custom_call" | custom-call | flops 21743271936 | bytes 66060288 | tf_op jit(solution)/shard_map/right/pallas_call | solution.py:207
  (39 shorter events, 24.0 us)
Async XLA Ops:
  6.5 174.6 %all-gather.2.cloned.1.call-start = ((), (), s32[]{:S(2)}) async-start(), calls=%async_computation | async-start | bytes 10616832 | tf_op jit(solution)/shard_map/all_gather | solution.py:268
  11.1 22.2 %collective-permute-start.3 = (f32[256,1536]{1,0:T(8,128)S(1)}, f32[256,1536]{1,0:T(8,128)}, u32[]{:S(2)}, u32[]{:S(2)}) collective-permute-start(f32[256,1536]{1,0:T(8,128)S(1)} %get-tuple-element.35), channel_id=1, source_target_pairs={{8,0},{16,8},{24,16},{9,1},{17,9},{25,17},{10,2},{18,10},{26,18},{... | collective-permute-start | bytes 4718600 | tf_op jit(solution)/shard_map/ppermute | solution.py:26
  13.7 20.4 %collective-permute-start.2 = (f32[256,1536]{1,0:T(8,128)S(1)}, f32[256,1536]{1,0:T(8,128)}, u32[]{:S(2)}, u32[]{:S(2)}) collective-permute-start(f32[256,1536]{1,0:T(8,128)S(1)} %get-tuple-element.36), channel_id=1, source_target_pairs={{0,8},{8,16},{16,24},{1,9},{9,17},{17,25},{2,10},{10,18},{18,26},{... | collective-permute-start | bytes 4718600 | tf_op jit(solution)/shard_map/ppermute | solution.py:25
  22.6 80.6 %collective-permute-start.1 = (f32[1536,256]{1,0:T(8,128)S(1)}, f32[1536,256]{1,0:T(8,128)S(1)}, u32[]{:S(2)}, u32[]{:S(2)}) collective-permute-start(f32[1536,256]{1,0:T(8,128)S(1)} %get-tuple-element.33), channel_id=1, source_target_pairs={{1,0},{2,1},{3,2},{4,3},{5,4},{6,5},{7,6},{9,8},{10,9},{11,10},{12... | collective-permute-start | bytes 4718600 | tf_op jit(solution)/shard_map/ppermute | solution.py:26
  25.5 78.8 %collective-permute-start = (f32[1536,256]{1,0:T(8,128)S(1)}, f32[1536,256]{1,0:T(8,128)}, u32[]{:S(2)}, u32[]{:S(2)}) collective-permute-start(f32[1536,256]{1,0:T(8,128)S(1)} %get-tuple-element.34), channel_id=1, source_target_pairs={{0,1},{1,2},{2,3},{3,4},{4,5},{5,6},{6,7},{8,9},{9,10},{10,11},{11... | collective-permute-start | bytes 4718600 | tf_op jit(solution)/shard_map/ppermute | solution.py:25
  103.1 1.2 copy-start.1
  182.2 7.2 %collective-permute-start.5 = (f32[1,384,128]{2,1,0:T(8,128)S(1)}, f32[1,384,128]{2,1,0:T(8,128)S(1)}, u32[]{:S(2)}, u32[]{:S(2)}) collective-permute-start(f32[1,384,128]{2,1,0:T(8,128)S(1)} %get-tuple-element.37), channel_id=1, source_target_pairs={{8,0},{16,8},{24,16},{9,1},{17,9},{25,17},{10,2},{18,10},{26,18},{... | collective-permute-start | bytes 589832 | tf_op jit(solution)/shard_map/ppermute | solution.py:26
  184.9 5.6 %collective-permute-start.4 = (f32[1,384,128]{2,1,0:T(8,128)S(1)}, f32[1,384,128]{2,1,0:T(8,128)S(1)}, u32[]{:S(2)}, u32[]{:S(2)}) collective-permute-start(f32[1,384,128]{2,1,0:T(8,128)S(1)} %get-tuple-element.38), channel_id=1, source_target_pairs={{0,8},{8,16},{16,24},{1,9},{9,17},{17,25},{2,10},{10,18},{18,26},{... | collective-permute-start | bytes 589832 | tf_op jit(solution)/shard_map/ppermute | solution.py:25
  189.3 1.2 copy-start.3
  190.5 0.7 copy-start.4
  207.6 77.2 %slice-start = ((s8[7864320]{0:T(1024)(128)(4,1)}), s8[4194304]{0:T(1024)(128)(4,1)S(1)}, s32[]{:S(2)}) async-start(s8[7864320]{0:T(1024)(128)(4,1)} %bitcast.9), calls=%async_computation.1 | async-start | bytes 8388608
  212.0 72.8 %collective-permute-start.6 = (f32[12,128,640]{2,1,0:T(8,128)}, f32[12,128,640]{2,1,0:T(8,128)}, u32[]{:S(2)}, u32[]{:S(2)}) collective-permute-start(f32[12,128,640]{2,1,0:T(8,128)} %dynamic-slice_select_fusion), channel_id=1, source_target_pairs={{0,16},{1,17},{10,26},{11,27},{20,4},{21,5},{30,14},{31,15}} | collective-permute-start | bytes 11796488 | tf_op jit(solution)/shard_map/ppermute | solution.py:253
  214.6 66.9 %collective-permute-start.7 = (f32[1536,256]{1,0:T(8,128)}, f32[1536,256]{1,0:T(8,128)}, u32[]{:S(2)}, u32[]{:S(2)}) collective-permute-start(f32[1536,256]{1,0:T(8,128)} %get-tuple-element.23), channel_id=1, source_target_pairs={{0,1},{1,2},{2,3},{3,4},{4,5},{5,6},{6,7},{8,9},{9,10},{10,11},{11... | collective-permute-start | bytes 4718600 | tf_op jit(solution)/shard_map/ppermute | solution.py:25
  216.6 68.2 %collective-permute-start.8 = (f32[1536,256]{1,0:T(8,128)}, f32[1536,256]{1,0:T(8,128)}, u32[]{:S(2)}, u32[]{:S(2)}) collective-permute-start(f32[1536,256]{1,0:T(8,128)} %get-tuple-element.24), channel_id=1, source_target_pairs={{1,0},{2,1},{3,2},{4,3},{5,4},{6,5},{7,6},{9,8},{10,9},{11,10},{12... | collective-permute-start | bytes 4718600 | tf_op jit(solution)/shard_map/ppermute | solution.py:26
  220.8 63.9 %slice-start.1 = ((s8[7864320]{0:T(1024)(128)(4,1)}), s8[3670016]{0:T(1024)(128)(4,1)S(1)}, s32[]{:S(2)}) async-start(s8[7864320]{0:T(1024)(128)(4,1)} %bitcast.9), calls=%async_computation.2 | async-start | bytes 7340032
  289.2 3.1 copy-start.2
  289.2 45.5 %collective-permute-start.11 = (f32[12,128,640]{2,1,0:T(8,128)}, f32[12,128,640]{2,1,0:T(8,128)}, u32[]{:S(2)}, u32[]{:S(2)}) collective-permute-start(f32[12,128,640]{2,1,0:T(8,128)} %fusion.2.held), channel_id=1, source_target_pairs={{0,8},{16,24},{1,9},{17,25},{10,2},{26,18},{11,3},{27,19},{4,12},{... | collective-permute-start | bytes 11796488 | tf_op jit(solution)/shard_map/ppermute | solution.py:253
  293.4 23.8 %collective-permute-start.10 = (f32[256,512]{1,0:T(8,128)}, f32[256,512]{1,0:T(8,128)}, u32[]{:S(2)}, u32[]{:S(2)}) collective-permute-start(f32[256,512]{1,0:T(8,128)} %slice.47), channel_id=1, source_target_pairs={{8,0},{16,8},{24,16},{9,1},{17,9},{25,17},{10,2},{18,10},{26,18},{... | collective-permute-start | bytes 1572872 | tf_op jit(solution)/shard_map/ppermute | solution.py:26
  301.6 1.7 copy-start
  304.2 13.0 %collective-permute-start.9 = (f32[256,512]{1,0:T(8,128)}, f32[256,512]{1,0:T(8,128)}, u32[]{:S(2)}, u32[]{:S(2)}) collective-permute-start(f32[256,512]{1,0:T(8,128)} %slice.46), channel_id=1, source_target_pairs={{0,8},{8,16},{16,24},{1,9},{9,17},{17,25},{2,10},{10,18},{18,26},{... | collective-permute-start | bytes 1572872 | tf_op jit(solution)/shard_map/ppermute | solution.py:25
Sparse Core Ops, SparseCore 0:
  9.5 171.5 all-gather.1
